TPU v7x, 32 devices: a whole 2x2x4 slice. The times are simulated.
32 devices in a mesh: replica: 4 (over y, core), fsdp: 8 (over z, x).
Axes of the slice: x: 2, y: 2, z: 4, core: 2. Of those that a mesh axis runs over, the one named last changes fastest.
Arguments:
- tokens_in: bfloat16 [4, 3072, 8192], P('replica', 'fsdp'), may hold values from -6 to 6
- targets: bfloat16 [4, 3072, 512], P('replica', 'fsdp'), may hold values from -6 to 6
- weights: float32 [4, 8192, 512], P('replica', 'fsdp'), may hold values from -6 to 6
- adam_mean: float32 [4, 8192, 512], P('replica', 'fsdp'), may hold values from -6 to 6
- adam_var: float32 [4, 8192, 512], P('replica', 'fsdp'), may hold values from 0.5 to 8
- anchor: float32 [8192, 512], P('fsdp'), may hold values from -6 to 6
- outer_momentum: float32 [8192, 512], P('fsdp'), may hold values from -6 to 6
- pseudo_grad: float32 [4, 8192, 128], P('replica', 'fsdp'), may hold values from -6 to 6
- fragment: int32 [], replicated, may hold values from 0 to 3
- delay: int32 [4], P('replica'), may hold values from 0 to 1, as said below
Outputs:
- new_weights: float32 [4, 8192, 512], P('replica', 'fsdp')
- new_adam_mean: float32 [4, 8192, 512], P('replica', 'fsdp')
- new_adam_var: float32 [4, 8192, 512], P('replica', 'fsdp')
- new_anchor: float32 [8192, 512], P('fsdp')
- new_momentum: float32 [8192, 512], P('fsdp')
Inputs may be any that keep to these rules, and one draw needn't show every extreme that they name: Exactly 2 of the workers have delay 1, the others 0.
All inputs are finite; a program needn't handle non-finite values.
Results may differ from a plain program's by a relative error of at most 0.00053.
Values may be sent and summed in bfloat16 or wider, within the bound.
A program may use at most 128 MiB of HBM per device.

v0:
```python
import math

import jax
import jax.numpy as jnp
from jax import lax
from jax.sharding import PartitionSpec as P

beta_first = 0.9
beta_second = 0.95
adam_epsilon = 1e-08
adam_steps = 20.0
inner_rate = 0.1
weight_decay = 0.1
outer_rate = 0.7
outer_pull = 0.9
blend_share = 0.5
norm_epsilon = 1e-05


def blend(field, anchor_next, offset):
    piece = lax.dynamic_slice_in_dim(field, offset, anchor_next.shape[1], 1)
    mixed = blend_share * anchor_next + (1.0 - blend_share) * piece
    return lax.dynamic_update_slice_in_dim(field, mixed, offset, 1)


def normalize(rows):
    wide = rows.astype(jnp.float32)
    stat = jnp.mean(wide * wide, axis=-1, keepdims=True)
    return (wide * lax.rsqrt(stat + norm_epsilon)).astype(jnp.bfloat16)


def adam_update(start_field, grad, first, second):
    mean_next = beta_first * first + (1.0 - beta_first) * grad
    var_next = beta_second * second + (1.0 - beta_second) * grad * grad
    first_fix = 1.0 - beta_first**adam_steps
    second_fix = 1.0 - beta_second**adam_steps
    ratio = mean_next / first_fix / (jnp.sqrt(var_next / second_fix) + adam_epsilon)
    return (start_field - inner_rate * (ratio + weight_decay * start_field), mean_next, var_next)


def on_device(
    tokens_in,
    targets,
    weights,
    adam_mean,
    adam_var,
    anchor,
    outer_momentum,
    pseudo_grad,
    fragment,
    delay,
):
    width = tokens_in.shape[2]
    tok_rows = tokens_in.shape[1]
    head_size = pseudo_grad.shape[2]
    total_tokens = tok_rows * lax.axis_size("fsdp")
    flag = delay[0]
    summed = lax.psum(pseudo_grad[0], "replica")
    average = summed / lax.axis_size("replica")
    offset = fragment * head_size
    anchor_piece = lax.dynamic_slice_in_dim(anchor, offset, head_size, 1)
    moment_piece = lax.dynamic_slice_in_dim(outer_momentum, offset, head_size, 1)
    moment_next = outer_pull * moment_piece + average
    anchor_next = anchor_piece - outer_rate * (average + outer_pull * moment_next)
    new_anchor = lax.dynamic_update_slice_in_dim(anchor, anchor_next, offset, 1)
    new_momentum = lax.dynamic_update_slice_in_dim(outer_momentum, moment_next, offset, 1)
    local = weights[0]
    merged = blend(local, anchor_next, offset)
    start_field = jnp.where(flag == 0, merged, local)
    normed = normalize(tokens_in[0])
    columns = normed
    keys = jnp.dot(
        columns,
        lax.all_gather(start_field.astype(jnp.bfloat16), "fsdp", axis=0, tiled=True),
        preferred_element_type=jnp.float32,
    )
    key_scale = 1.0 / math.sqrt(width)
    residual = (keys * key_scale - targets[0].astype(jnp.float32)).astype(jnp.bfloat16)
    columns = normed
    grad = lax.psum_scatter(
        lax.dot_general(
            columns, residual, (((0,), (0,)), ((), ())), preferred_element_type=jnp.float32
        ),
        "fsdp",
        scatter_dimension=0,
        tiled=True,
    )
    grad = grad * (1.0 / math.sqrt(total_tokens))
    stepped, mean_next, var_next = adam_update(start_field, grad, adam_mean[0], adam_var[0])
    finished = jnp.where(flag == 1, blend(stepped, anchor_next, offset), stepped)
    return (finished[None], mean_next[None], var_next[None], new_anchor, new_momentum)


def solution(mesh):
    in_specs = (
        P("replica", "fsdp", None),
        P("replica", "fsdp", None),
        P("replica", "fsdp", None),
        P("replica", "fsdp", None),
        P("replica", "fsdp", None),
        P("fsdp", None),
        P("fsdp", None),
        P("replica", "fsdp", None),
        P(),
        P("replica"),
    )
    out_specs = (
        P("replica", "fsdp", None),
        P("replica", "fsdp", None),
        P("replica", "fsdp", None),
        P("fsdp", None),
        P("fsdp", None),
    )
    return jax.shard_map(
        on_device, mesh=mesh, in_specs=in_specs, out_specs=out_specs, check_vma=False
    )
```

profile of v0, /device:TPU:0, one launch (start us, length us, event | category | flops | bytes accessed | tf_op | source)
XLA Modules:
  0.0 493.2 jit_solution(6436693503603833739)
XLA Ops:
  7.2 0.0 copy-start
  7.2 0.0 all-reduce.2.cloned.1.call-start
  7.2 3.2 copy.25
  10.4 0.0 copy-done
  10.4 1.3 copy.26
  11.8 0.0 all-reduce.2.cloned.1.call-update
  11.8 0.0 all-gather.2.cloned.1.call-start
  13.1 1.6 copy.18
  14.7 33.1 %all-reduce.2.cloned.1.call-done = f32[1024,128]{1,0:T(8,128)} async-done(((f32[1024,128]{1,0:T(8,128)}), f32[1024,128]{1,0:T(8,128)}) %all-reduce.2.cloned.1.call-update) | async-done | bytes 524304 | tf_op jit(solution)/shard_map/psum | solution.py:58
  47.8 2.5 constant_dynamic-update-slice_fusion
  50.3 1.1 fusion.17
  51.5 1.1 convert_element_type.24
  52.6 0.0 all-gather.2.cloned.1.call-update
  52.6 0.0 copy-start.2
  52.6 0.0 reduce-scatter.2.cloned.1.call-start
  52.7 4.1 fusion
  56.8 120.9 %all-gather.2.cloned.1.call-done = bf16[8192,512]{1,0:T(8,128)(2,1)} async-done(((bf16[1024,512]{1,0:T(8,128)(2,1)}), bf16[8192,512]{1,0:T(8,128)(2,1)}) %all-gather.2.cloned.1.call-update) | async-done | bytes 8388624 | tf_op jit(solution)/shard_map/all_gather | solution.py:74
  177.7 0.0 copy-done.2
  177.7 8.7 %fusion.12 = bf16[384,512]{1,0:T(8,128)(2,1)S(1)} fusion(bf16[8192,512]{1,0:T(8,128)(2,1)} %all-gather.2.cloned.1.call-done, bf16[1,384,8192]{2,1,0:T(8,128)(2,1)} %param.10, f32[384]{0:T(512)S(1)} %add_rsqrt_fusion, bf16[1,384,512]{2,1,0:T(8,128)(2,1)S(1)} %copy-done.2), kind=kOutput, calls=%fused_computation.11 | convolution fusion | flops 3231449088 | bytes 15468032 | tf_op jit(solution)/shard_map/dot_general | solution.py:72
  186.3 11.3 %fusion.2 = f32[8192,512]{1,0:T(8,128)} fusion(bf16[384,512]{1,0:T(8,128)(2,1)S(1)} %fusion.12, bf16[1,384,8192]{2,1,0:T(8,128)(2,1)} %param.10, f32[384]{0:T(512)S(1)} %add_rsqrt_fusion), kind=kOutput, calls=%fused_computation.4 | convolution fusion | flops 3230662656 | bytes 23463424 | tf_op jit(solution)/shard_map/dot_general | solution.py:81
  197.6 0.0 reduce-scatter.2.cloned.1.call-update
  197.6 281.0 %reduce-scatter.2.cloned.1.call-done = f32[1024,512]{1,0:T(8,128)} async-done(((f32[8192,512]{1,0:T(8,128)}), f32[1024,512]{1,0:T(8,128)}) %reduce-scatter.2.cloned.1.call-update) | async-done | bytes 2097168 | tf_op jit(solution)/shard_map/reduce_scatter | solution.py:80
  478.6 6.5 %fusion.18 = (f32[1,1024,512]{2,1,0:T(8,128)}, f32[1024,512]{1,0:T(8,128)S(1)}, f32[1,1024,512]{2,1,0:T(8,128)}) fusion(f32[1024,512]{1,0:T(8,128)} %reduce-scatter.2.cloned.1.call-done, f32[1,1024,512]{2,1,0:T(8,128)} %param.14, f32[1024,512]{1,0:T(8,128)S(1)} %fusion.17, f32[1,1024,512]{2,1,0:T(8,128)} %param.13), kind=kLoop, calls=%fused_computation.20 | loop fusion | flops 8388608 | bytes 14680064 | tf_op jit(solution)/shard_map/broadcast_in_dim | solution.py:91
  485.1 0.2 copy.19
  485.3 0.1 bitcast_dynamic-update-slice_fusion
  485.4 0.0 copy-start.1
  485.4 1.3 copy-done.1
  (1 shorter events, 0.0 us)
Async XLA Ops:
  7.2 3.3 copy-start
  7.2 40.7 %all-reduce.2.cloned.1.call-start = ((), (), s32[]{:S(2)}) async-start(), calls=%async_computation.1 | async-start | bytes 1048576 | tf_op jit(solution)/shard_map/psum | solution.py:58
  11.8 165.9 %all-gather.2.cloned.1.call-start = ((), (), s32[]{:S(2)}) async-start(), calls=%async_computation.2 | async-start | bytes 9437184 | tf_op jit(solution)/shard_map/all_gather | solution.py:74
  52.6 125.1 %copy-start.2 = (bf16[1,384,512]{2,1,0:T(8,128)(2,1)S(1)}, bf16[1,384,512]{2,1,0:T(8,128)(2,1)}, u32[]{:S(2)}) copy-start(bf16[1,384,512]{2,1,0:T(8,128)(2,1)} %param.11) | copy-start | bytes 1179652
  52.6 426.0 %reduce-scatter.2.cloned.1.call-start = ((), (), s32[]{:S(2)}) async-start(), calls=%async_computation.3 | async-start | bytes 18874368 | tf_op jit(solution)/shard_map/reduce_scatter | solution.py:80
  485.4 1.3 copy-start.1
Sparse Core Ops, SparseCore 0:
  11.9 35.8 all-reduce.1
  52.7 124.9 all-gather.1
  197.7 280.7 reduce-scatter.1
where the time goes:
time: 494 us; the launch traced here: 493 us
  waiting for transfers between devices  435 us (88%)
  matrix products  19.9 us (4%)
  other arithmetic  15.5 us (3%)
  between operations  15.1 us (3%)
  local copies, waits for them, and re-layouts  7.63 us (2%)
    reduce_scatter x1, waiting for transfers between devices, on_device(): lax.psum_scatter(lax.dot_general(columns, residual, (((0,), (0,)), ((), (...  281 us
    all_gather x1, waiting for transfers between devices, on_device(): lax.all_gather(start_field.astype(jnp.bfloat16), 'fsdp', axis=0, tiled=True)  121 us
    psum x1, waiting for transfers between devices, on_device(): summed = lax.psum(pseudo_grad[0], 'replica')  33.1 us
    dot_general x1, matrix products, on_device(): lax.dot_general(columns, residual, (((0,), (0,)), ((), ())), preferred_el...  11.3 us
  transfers between devices with their start and end apart: 3, of which 3 were waited for; matrix products, arithmetic and copies ran while one was open for 1% of the time, Pallas kernels for 0%

commit v1 on v0

v1 whole, which is shorter than its diff:
```python
import functools
import math

import jax
import jax.numpy as jnp
from jax import lax
from jax.experimental import pallas as pl
from jax.experimental.pallas import tpu as pltpu
from jax.sharding import PartitionSpec as P

beta_first = 0.9
beta_second = 0.95
adam_epsilon = 1e-08
adam_steps = 20.0
inner_rate = 0.1
weight_decay = 0.1
outer_rate = 0.7
outer_pull = 0.9
blend_share = 0.5
norm_epsilon = 1e-05

GROUP = 4
ROW_PARTS = 4
MESH = pl.DeviceIdType.MESH


def adam_update(start_field, grad, first, second):
    mean_next = beta_first * first + (1.0 - beta_first) * grad
    var_next = beta_second * second + (1.0 - beta_second) * grad * grad
    first_fix = 1.0 - beta_first**adam_steps
    second_fix = 1.0 - beta_second**adam_steps
    ratio = mean_next / first_fix / (jnp.sqrt(var_next / second_fix) + adam_epsilon)
    return (start_field - inner_rate * (ratio + weight_decay * start_field), mean_next, var_next)


def tile_of(extent, most):
    tile = min(extent, most)
    while extent % tile:
        tile //= 2
    return tile


def kernel(
    n_rep, n_fsdp,
    frag_ref, delay_ref, tokens_h, targets_h, weights_h, mean_h, var_h, anchor_h, moment_h, pg_h,
    weights_o, mean_o, var_o, anchor_o, moment_o,
    tin, tok, tgt, wf, wb, mean, var, anc, mom, pgs, kp, kin, rbuf, gbuf, gin,
    load_sem, tload_sem, out_sem,
    pg_ss, pg_rs, t_ss, t_rs, w_ss, w_rs, k_ss, k_rs, r_ss, r_rs, g_ss, g_rs,
):
    rows, width = tin.shape
    blk, kw = wf.shape
    head = pgs.shape[2]
    chunks = kw // head
    quads = n_fsdp // GROUP
    part = rows // ROW_PARTS
    me = lax.axis_index("fsdp")
    rep = lax.axis_index("replica")
    g = lax.rem(me, GROUP)
    q = lax.div(me, GROUP)

    def member(d):
        return lax.rem(g + d, GROUP)

    def quad(e):
        return lax.rem(q + e, quads)

    def to_member(d):
        return (rep, q * GROUP + member(d))

    def to_quad(e):
        return (rep, quad(e) * GROUP + g)

    def to_replica(d):
        return (lax.rem(rep + d, n_rep), me)

    def remote(src, dst, ss, rs, where):
        return pltpu.make_async_remote_copy(
            src_ref=src, dst_ref=dst, send_sem=ss, recv_sem=rs, device_id=where, device_id_type=MESH
        )

    loads = []
    for k in range(ROW_PARTS):
        span = pl.ds(k * part, part)
        loads.append(pltpu.make_async_copy(tokens_h.at[span], tin.at[span], tload_sem.at[k]))
        loads[-1].start()
    pairs = [
        (pg_h, pgs.at[rep]), (weights_h, wf), (anchor_h, anc), (moment_h, mom),
        (targets_h, tgt), (mean_h, mean), (var_h, var),
    ]
    more = []
    for i, (src, dst) in enumerate(pairs):
        more.append(pltpu.make_async_copy(src, dst, load_sem.at[i]))
        more[-1].start()

    peers = [to_replica(d) for d in range(1, n_rep)]
    peers += [to_member(d) for d in range(1, GROUP)]
    peers += [to_quad(e) for e in range(1, quads)]
    barrier = pltpu.get_barrier_semaphore()
    for where in peers:
        pl.semaphore_signal(barrier, inc=1, device_id=where, device_id_type=MESH)
    pl.semaphore_wait(barrier, len(peers))

    sent = []

    more[0].wait()
    pg_copies = []
    for d in range(1, n_rep):
        copy = remote(pgs.at[rep], pgs.at[rep], pg_ss.at[d - 1], pg_rs.at[d - 1], to_replica(d))
        copy.start()
        sent.append(copy)
        source = lax.rem(rep + n_rep - d, n_rep)
        pg_copies.append(
            remote(pgs.at[source], pgs.at[source], pg_ss.at[d - 1], pg_rs.at[d - 1], to_replica(d))
        )

    my_rows = pl.multiple_of(g * rows, 128)
    lane = 128
    for k in range(ROW_PARTS):
        loads[k].wait()

        def norm(i, _, k=k):
            at = pl.ds(pl.multiple_of(k * part + i * 16, 16), 16)
            total = jnp.zeros((16, lane), jnp.float32)
            for j in range(width // lane):
                v = tin[at, j * lane:(j + 1) * lane].astype(jnp.float32)
                total = total + v * v
            stat = jnp.sum(total, axis=-1, keepdims=True) * (1.0 / width)
            scale = jnp.broadcast_to(lax.rsqrt(stat + norm_epsilon), (16, lane))
            for j in range(width // lane):
                cols = slice(j * lane, (j + 1) * lane)
                tin[at, cols] = (tin[at, cols].astype(jnp.float32) * scale).astype(jnp.bfloat16)
            return 0

        lax.fori_loop(0, part // 16, norm, 0)
        span = pl.ds(k * part, part)
        dst_rows = pl.ds(pl.multiple_of(my_rows + k * part, 16), part)
        for d in range(1, GROUP):
            for j in range(quads):
                cols = pl.ds(pl.multiple_of((j * GROUP + member(d)) * blk, 128), blk)
                copy = remote(
                    tin.at[span, cols], tok.at[dst_rows, pl.ds(j * blk, blk)],
                    t_ss.at[k, d - 1, j], t_rs.at[k, d - 1, j], to_member(d),
                )
                copy.start()
                sent.append(copy)
        for j in range(quads):
            cols = pl.ds(pl.multiple_of((j * GROUP + g) * blk, 128), blk)
            tok[dst_rows, j * blk:(j + 1) * blk] = tin[span, cols]

    for copy in more[1:4]:
        copy.wait()
    for copy in pg_copies:
        copy.wait_recv()
    frag = frag_ref[0]
    flag = delay_ref[0]
    step_rows = tile_of(blk, 128)

    def outer(i, _):
        at = pl.ds(pl.multiple_of(i * step_rows, step_rows), step_rows)
        shape = (step_rows, head)
        total = pgs[0, at, :]
        for r in range(1, n_rep):
            total = total + pgs[r, at, :]
        average = total / n_rep
        frag_v = jnp.full(shape, frag, jnp.int32)
        flag_v = jnp.full(shape, flag, jnp.int32)
        for h in range(chunks):
            cols = slice(h * head, (h + 1) * head)
            mine = frag_v == h
            old_m, old_a, old_w = mom[at, cols], anc[at, cols], wf[at, cols]
            moment_next = outer_pull * old_m + average
            anchor_next = old_a - outer_rate * (average + outer_pull * moment_next)
            mom[at, cols] = jnp.where(mine, moment_next, old_m)
            anc[at, cols] = jnp.where(mine, anchor_next, old_a)
            mixed = blend_share * anchor_next + (1.0 - blend_share) * old_w
            start = jnp.where(mine & (flag_v == 0), mixed, old_w)
            wf[at, cols] = start
            wb[h, pl.ds(pl.multiple_of(q * blk + i * step_rows, step_rows), step_rows), :] = start.astype(jnp.bfloat16)
        return 0

    lax.fori_loop(0, blk // step_rows, outer, 0)
    w_copies = []
    for c in range(chunks):
        own = wb.at[c, pl.ds(pl.multiple_of(q * blk, 128), blk)]
        for e in range(1, quads):
            copy = remote(own, own, w_ss.at[c, e - 1], w_rs.at[c, e - 1], to_quad(e))
            copy.start()
            sent.append(copy)
    outs = []

    def put(src, dst):
        copy = pltpu.make_async_copy(src, dst, out_sem.at[len(outs)])
        copy.start()
        outs.append(copy)

    put(anc, anchor_o)
    put(mom, moment_o)

    key_scale = 1.0 / math.sqrt(width)
    grad_scale = 1.0 / math.sqrt(rows * n_fsdp)

    def rows_of(p):
        return pl.ds(pl.multiple_of(p * rows, 128), rows)

    def keys_of(c):
        for e in range(1, quads):
            at = wb.at[c, pl.ds(pl.multiple_of(quad(quads - e) * blk, 128), blk)]
            remote(at, at, w_ss.at[c, e - 1], w_rs.at[c, e - 1], to_quad(e)).wait_recv()
        for d in (1, 2, 3, 0):
            p = member(d)
            if c == 0 and d:
                for k in range(ROW_PARTS):
                    for j in range(quads):
                        at = tok.at[pl.ds(pl.multiple_of(p * rows + k * part, 16), part), pl.ds(j * blk, blk)]
                        remote(
                            at, at, t_ss.at[k, GROUP - d - 1, j], t_rs.at[k, GROUP - d - 1, j], to_member(d)
                        ).wait_recv()
            kp[c, d] = jnp.dot(tok[rows_of(p), :], wb[c], preferred_element_type=jnp.float32)
            if d:
                copy = remote(kp.at[c, d], kin.at[c, d - 1], k_ss.at[c, d - 1], k_rs.at[c, d - 1], to_member(d))
                copy.start()
                sent.append(copy)

    def residual_of(c):
        if c == 0:
            more[4].wait()
        for d in range(1, GROUP):
            remote(kp.at[c, d], kin.at[c, d - 1], k_ss.at[c, d - 1], k_rs.at[c, d - 1], to_member(d)).wait_recv()
        for i in range(rows // 128):
            at = slice(i * 128, (i + 1) * 128)
            keys = kp[c, 0, at, :]
            for d in range(1, GROUP):
                keys = keys + kin[c, d - 1, at, :]
            wide = keys * key_scale - tgt[at, c * head:(c + 1) * head].astype(jnp.float32)
            rbuf[c, :, pl.ds(pl.multiple_of(my_rows + i * 128, 128), 128)] = wide.T.astype(jnp.bfloat16)
        own = rbuf.at[c, :, rows_of(g)]
        for d in range(1, GROUP):
            copy = remote(own, own, r_ss.at[c, d - 1], r_rs.at[c, d - 1], to_member(d))
            copy.start()
            sent.append(copy)

    tile = tile_of(blk, 256)

    def grad_of(c):
        for d in range(1, GROUP):
            at = rbuf.at[c, :, rows_of(member(GROUP - d))]
            remote(at, at, r_ss.at[c, d - 1], r_rs.at[c, d - 1], to_member(d)).wait_recv()
        for e in list(range(1, quads)) + [0]:
            j = quad(e)

            def piece(i, _, j=j, e=e):
                cols = pl.ds(pl.multiple_of(j * blk + i * tile, tile), tile)
                gbuf[c, e, :, pl.ds(pl.multiple_of(i * tile, tile), tile)] = jnp.dot(
                    rbuf[c], tok[:, cols], preferred_element_type=jnp.float32
                )
                return 0

            lax.fori_loop(0, blk // tile, piece, 0)
            if e:
                copy = remote(gbuf.at[c, e], gin.at[c, e - 1], g_ss.at[c, e - 1], g_rs.at[c, e - 1], to_quad(e))
                copy.start()
                sent.append(copy)

    def finish(c):
        if c == 0:
            more[5].wait()
            more[6].wait()
        for e in range(1, quads):
            remote(gbuf.at[c, e], gin.at[c, e - 1], g_ss.at[c, e - 1], g_rs.at[c, e - 1], to_quad(e)).wait_recv()
        cols = slice(c * head, (c + 1) * head)

        def piece(i, _):
            at = pl.ds(pl.multiple_of(i * 128, 128), 128)
            total = gbuf[c, 0, :, at]
            for e in range(1, quads):
                total = total + gin[c, e - 1, :, at]
            grad = total.T * grad_scale
            stepped, mean_next, var_next = adam_update(wf[at, cols], grad, mean[at, cols], var[at, cols])
            mean[at, cols] = mean_next
            var[at, cols] = var_next
            mixed = blend_share * anc[at, cols] + (1.0 - blend_share) * stepped
            shape = (128, head)
            late = (jnp.full(shape, frag, jnp.int32) == c) & (jnp.full(shape, flag, jnp.int32) == 1)
            wf[at, cols] = jnp.where(late, mixed, stepped)
            return 0

        lax.fori_loop(0, blk // 128, piece, 0)
        put(wf.at[:, cols], weights_o.at[:, cols])
        put(mean.at[:, cols], mean_o.at[:, cols])
        put(var.at[:, cols], var_o.at[:, cols])

    keys_of(0)
    for c in range(chunks):
        residual_of(c)
        if c + 1 < chunks:
            keys_of(c + 1)
        grad_of(c)
        if c >= 2:
            finish(c - 2)
    for c in range(max(chunks - 2, 0), chunks):
        finish(c)
    for copy in sent:
        copy.wait_send()
    for copy in outs:
        copy.wait()


def on_device(n_rep, n_fsdp, tokens_in, targets, weights, adam_mean, adam_var, anchor, outer_momentum, pseudo_grad, fragment, delay):
    rows, width = tokens_in.shape[1:]
    blk, kw = weights.shape[1:]
    head = pseudo_grad.shape[2]
    chunks = kw // head
    quads = n_fsdp // GROUP
    f32, bf16 = jnp.float32, jnp.bfloat16
    state = jax.ShapeDtypeStruct((blk, kw), f32)
    hbm = pl.BlockSpec(memory_space=pl.ANY)
    smem = pl.BlockSpec(memory_space=pltpu.SMEM)
    dma = pltpu.SemaphoreType.DMA
    out = pl.pallas_call(
        functools.partial(kernel, n_rep, n_fsdp),
        out_shape=[state] * 5,
        in_specs=[smem] * 2 + [hbm] * 8,
        out_specs=[hbm] * 5,
        scratch_shapes=[
            pltpu.VMEM((rows, width), bf16),
            pltpu.VMEM((GROUP * rows, quads * blk), bf16),
            pltpu.VMEM((rows, kw), bf16),
            pltpu.VMEM((blk, kw), f32),
            pltpu.VMEM((chunks, quads * blk, head), bf16),
            pltpu.VMEM((blk, kw), f32),
            pltpu.VMEM((blk, kw), f32),
            pltpu.VMEM((blk, kw), f32),
            pltpu.VMEM((blk, kw), f32),
            pltpu.VMEM((n_rep, blk, head), f32),
            pltpu.VMEM((chunks, GROUP, rows, head), f32),
            pltpu.VMEM((chunks, GROUP - 1, rows, head), f32),
            pltpu.VMEM((chunks, head, GROUP * rows), bf16),
            pltpu.VMEM((chunks, quads, head, blk), f32),
            pltpu.VMEM((chunks, quads - 1, head, blk), f32),
            dma((7,)), dma((ROW_PARTS,)), dma((2 + 3 * chunks,)),
            dma((n_rep - 1,)), dma((n_rep - 1,)),
            dma((ROW_PARTS, GROUP - 1, quads)), dma((ROW_PARTS, GROUP - 1, quads)),
            dma((chunks, quads - 1)), dma((chunks, quads - 1)),
            dma((chunks, GROUP - 1)), dma((chunks, GROUP - 1)),
            dma((chunks, GROUP - 1)), dma((chunks, GROUP - 1)),
            dma((chunks, quads - 1)), dma((chunks, quads - 1)),
        ],
        compiler_params=pltpu.CompilerParams(
            collective_id=0, has_side_effects=True, vmem_limit_bytes=60 * 2**20
        ),
        cost_estimate=pl.CostEstimate(
            flops=4 * rows * width * kw, bytes_accessed=2 * rows * width + 40 * blk * kw, transcendentals=blk * kw
        ),
    )(
        fragment.reshape(1), delay, tokens_in[0], targets[0], weights[0], adam_mean[0], adam_var[0],
        anchor, outer_momentum, pseudo_grad[0],
    )
    return (out[0][None], out[1][None], out[2][None], out[3], out[4])


def solution(mesh):
    split = P("replica", "fsdp", None)
    return jax.shard_map(
        functools.partial(on_device, mesh.shape["replica"], mesh.shape["fsdp"]),
        mesh=mesh,
        in_specs=(split,) * 5 + (P("fsdp", None),) * 2 + (split, P(), P("replica")),
        out_specs=(split,) * 3 + (P("fsdp", None),) * 2,
        check_vma=False,
    )
```

time: 494 us -> 226 us (0.46)
  waiting for transfers between devices: 435 us -> 0 us
  Pallas kernels: 0 us -> 212 us
  matrix products: 19.9 us -> 0 us
  other arithmetic: 15.5 us -> 0 us
  between operations: 15.1 us -> 1.95 us
    reduce_scatter x1 -> x0, waiting for transfers between devices: 281 us -> none  [on_device(): lax.psum_scatter(lax.dot_general(columns, residual, (((0,), (0,)), ((), (...]
    pallas_call x0 -> x1, Pallas kernels: none -> 212 us  [on_device(): pl.pallas_call(functools.partial(kernel, n_rep, n_fsdp), out_shape=[state...]
    all_gather x1 -> x0, waiting for transfers between devices: 121 us -> none  [on_device(): lax.all_gather(start_field.astype(jnp.bfloat16), 'fsdp', axis=0, tiled=True)]
    psum x1 -> x0, waiting for transfers between devices: 33.1 us -> none  [on_device(): summed = lax.psum(pseudo_grad[0], 'replica')]
    dot_general x2 -> x0, matrix products: 19.9 us -> none  [the longest x1 11.3 us: on_device(): lax.dot_general(columns, residual, (((0,), (0,)), ((), ())), preferred_el...]
    broadcast_in_dim x1 -> x0, other arithmetic: 6.52 us -> none  [on_device(): var_next[None]]
    unnamed x10 -> x13, local copies, waits for them, and re-layouts: 7.63 us -> 11.6 us
  transfers between devices with their start and end apart: 3 -> 0, of which waited for: 3 -> 0; matrix products, arithmetic and copies ran while one was open for 1% -> 0% of each run, Pallas kernels for 0% -> 0%
where the time goes in v1:
time: 226 us; the launch traced here: 225 us
  Pallas kernels  212 us (94%)
  local copies, waits for them, and re-layouts  11.6 us (5%)
    pallas_call x1, Pallas kernels, on_device(): pl.pallas_call(functools.partial(kernel, n_rep, n_fsdp), out_shape=[state...  212 us
    unnamed x13, local copies, waits for them, and re-layouts  11.6 us

profile of v1, /device:TPU:0, one launch (start us, length us, event | category | flops | bytes accessed | tf_op | source)
XLA Modules:
  0.0 225.3 jit_solution(5915288006513407134)
XLA Ops:
  1.9 211.8 %shard_map.137 = (f32[1024,512]{1,0:T(8,128)}, f32[1024,512]{1,0:T(8,128)}, f32[1024,512]{1,0:T(8,128)}, f32[1024,512]{1,0:T(8,128)}, f32[1024,512]{1,0:T(8,128)}) custom-call(s32[1]{0:T(128)} %bitcast.10.frag_ref, s32[1]{0:T(128)S(6)} %copy.21.delay_ref, bf16[384,8192]{1,0:T(8,128)(2,1)} %bitcast.14, bf16[384,512]{1,0:T(8,128)(2,1)} %bitcast.19, ...), custom_call_target="tpu_custom_call" | custom-call | flops 6442450944 | bytes 27262976 | tf_op jit(solution)/shard_map/pallas_call | solution.py:320
  213.7 0.0 copy-start.3
  213.7 3.2 %copy.22 = f32[1,1024,512]{2,1,0:T(8,128)} copy(f32[1,1024,512]{2,1,0:T(8,128)} %bitcast.13) | data formatting | bytes 4194304
  217.0 0.0 copy-done.3
  217.0 0.0 copy-start.2
  217.0 1.3 copy.23
  218.3 1.0 copy-done.2
  219.3 0.0 copy-start.1
  219.3 1.3 copy.24
  220.6 1.0 copy-done.1
  221.7 0.0 copy-start
  221.7 1.3 copy.25
  223.0 1.0 copy-done
  224.0 1.3 copy.26
Async XLA Ops:
  213.7 3.2 %copy-start.3 = (f32[1024,512]{1,0:T(8,128)S(1)}, f32[1024,512]{1,0:T(8,128)}, u32[]{:S(2)}) copy-start(f32[1024,512]{1,0:T(8,128)} %get-tuple-element.11) | copy-start | bytes 6291460
  217.0 2.3 %copy-start.2 = (f32[1024,512]{1,0:T(8,128)S(1)}, f32[1024,512]{1,0:T(8,128)}, u32[]{:S(2)}) copy-start(f32[1024,512]{1,0:T(8,128)} %get-tuple-element.12) | copy-start | bytes 6291460
  219.3 2.3 %copy-start.1 = (f32[1024,512]{1,0:T(8,128)S(1)}, f32[1024,512]{1,0:T(8,128)}, u32[]{:S(2)}) copy-start(f32[1024,512]{1,0:T(8,128)} %get-tuple-element.23) | copy-start | bytes 6291460
  221.7 2.3 %copy-start = (f32[1024,512]{1,0:T(8,128)S(1)}, f32[1024,512]{1,0:T(8,128)}, u32[]{:S(2)}) copy-start(f32[1024,512]{1,0:T(8,128)} %get-tuple-element.24) | copy-start | bytes 6291460

commit v2 on v1

--- a/solution.py
+++ b/solution.py
@@ -40,11 +40,34 @@
     return tile
 
 
+def coded(values):
+    top = values.astype(jnp.bfloat16)
+    wide = top.astype(jnp.float32)
+    rest = (values - wide) * (512.0 / jnp.maximum(jnp.abs(wide), 1e-30))
+    digit = jnp.clip(jnp.floor(rest), -2.0, 1.0) + 2.0
+    n = values.shape[0] // 4
+    low = digit[:n] * 64.0 + digit[n:2 * n] * 16.0 + digit[2 * n:3 * n] * 4.0 + digit[3 * n:] - 128.0
+    return top, low.astype(jnp.bfloat16)
+
+
+def decoded(top, low):
+    wide = top.astype(jnp.float32)
+    left = low.astype(jnp.float32) + 128.0
+    digits = []
+    for unit in (64.0, 16.0, 4.0):
+        digit = jnp.floor(left * (1.0 / unit))
+        left = left - unit * digit
+        digits.append(digit)
+    digits.append(left)
+    digit = jnp.concatenate(digits, axis=0)
+    return wide + jnp.abs(wide) * ((digit - 1.5) * (1.0 / 512.0))
+
+
 def kernel(
     n_rep, n_fsdp,
     frag_ref, delay_ref, tokens_h, targets_h, weights_h, mean_h, var_h, anchor_h, moment_h, pg_h,
     weights_o, mean_o, var_o, anchor_o, moment_o,
-    tin, tok, tgt, wf, wb, mean, var, anc, mom, pgs, kp, kin, rbuf, gbuf, gin,
+    tin, tok, tgt, wf, wb, mean, var, anc, mom, pgs, kp, kin, rbuf, gown, gbuf, gin,
     load_sem, tload_sem, out_sem,
     pg_ss, pg_rs, t_ss, t_rs, w_ss, w_rs, k_ss, k_rs, r_ss, r_rs, g_ss, g_rs,
 ):
@@ -59,6 +82,9 @@
     g = lax.rem(me, GROUP)
     q = lax.div(me, GROUP)
 
+    x = lax.rem(g, 2)
+    places = (g, g + 1 - 2 * x, lax.rem(g + 2, GROUP), lax.rem(g + 3 - 2 * x, GROUP))
+
     def member(d):
         return lax.rem(g + d, GROUP)
 
@@ -67,6 +93,9 @@
 
     def to_member(d):
         return (rep, q * GROUP + member(d))
+
+    def to_place(i):
+        return (rep, q * GROUP + places[i])
 
     def to_quad(e):
         return (rep, quad(e) * GROUP + g)
@@ -116,10 +145,10 @@
 
     my_rows = pl.multiple_of(g * rows, 128)
     lane = 128
-    for k in range(ROW_PARTS):
+    def send_tokens(k):
         loads[k].wait()
 
-        def norm(i, _, k=k):
+        def norm(i, _):
             at = pl.ds(pl.multiple_of(k * part + i * 16, 16), 16)
             total = jnp.zeros((16, lane), jnp.float32)
             for j in range(width // lane):
@@ -147,6 +176,9 @@
         for j in range(quads):
             cols = pl.ds(pl.multiple_of((j * GROUP + g) * blk, 128), blk)
             tok[dst_rows, j * blk:(j + 1) * blk] = tin[span, cols]
+
+    for k in range(ROW_PARTS // 2):
+        send_tokens(k)
 
     for copy in more[1:4]:
         copy.wait()
@@ -187,6 +219,8 @@
             copy = remote(own, own, w_ss.at[c, e - 1], w_rs.at[c, e - 1], to_quad(e))
             copy.start()
             sent.append(copy)
+    for k in range(ROW_PARTS // 2, ROW_PARTS):
+        send_tokens(k)
     outs = []
 
     def put(src, dst):
@@ -203,78 +237,101 @@
     def rows_of(p):
         return pl.ds(pl.multiple_of(p * rows, 128), rows)
 
-    def keys_of(c):
+    def exchange(src, dst, ss, rs, c, i, place):
+        return remote(src, dst, ss.at[c, i], rs.at[c, i], to_place(place))
+
+    def start(copy):
+        copy.start()
+        sent.append(copy)
+
+    def key_parts(c):
         for e in range(1, quads):
             at = wb.at[c, pl.ds(pl.multiple_of(quad(quads - e) * blk, 128), blk)]
             remote(at, at, w_ss.at[c, e - 1], w_rs.at[c, e - 1], to_quad(e)).wait_recv()
-        for d in (1, 2, 3, 0):
-            p = member(d)
-            if c == 0 and d:
+        if c == 0:
+            for d in range(1, GROUP):
                 for k in range(ROW_PARTS):
                     for j in range(quads):
-                        at = tok.at[pl.ds(pl.multiple_of(p * rows + k * part, 16), part), pl.ds(j * blk, blk)]
+                        at = tok.at[pl.ds(pl.multiple_of(member(d) * rows + k * part, 16), part), pl.ds(j * blk, blk)]
                         remote(
                             at, at, t_ss.at[k, GROUP - d - 1, j], t_rs.at[k, GROUP - d - 1, j], to_member(d)
                         ).wait_recv()
-            kp[c, d] = jnp.dot(tok[rows_of(p), :], wb[c], preferred_element_type=jnp.float32)
-            if d:
-                copy = remote(kp.at[c, d], kin.at[c, d - 1], k_ss.at[c, d - 1], k_rs.at[c, d - 1], to_member(d))
-                copy.start()
-                sent.append(copy)
+        for i in (3, 1, 2, 0):
+            kp[c, i] = jnp.dot(tok[rows_of(places[i]), :], wb[c], preferred_element_type=jnp.float32)
+
+    def key_copy(c, i):
+        return exchange(kp.at[c, (3, 1, 2)[i]], kin.at[c, i], k_ss, k_rs, c, i, (1, 1, 2)[i])
+
+    def send_keys(c):
+        for i in range(2):
+            start(key_copy(c, i))
+
+    def pass_keys(c):
+        key_copy(c, 0).wait_recv()
+        kp[c, 2] = kp[c, 2] + kin[c, 0]
+        start(key_copy(c, 2))
+
+    def residual_copy(c, i, arrived=False):
+        at = rows_of(places[(2, 1, 3)[i] if arrived else (0, 0, 2)[i]])
+        return exchange(rbuf.at[c, :, at], rbuf.at[c, :, at], r_ss, r_rs, c, i, (2, 1, 1)[i])
 
     def residual_of(c):
         if c == 0:
             more[4].wait()
-        for d in range(1, GROUP):
-            remote(kp.at[c, d], kin.at[c, d - 1], k_ss.at[c, d - 1], k_rs.at[c, d - 1], to_member(d)).wait_recv()
+        key_copy(c, 1).wait_recv()
+        key_copy(c, 2).wait_recv()
         for i in range(rows // 128):
             at = slice(i * 128, (i + 1) * 128)
-            keys = kp[c, 0, at, :]
-            for d in range(1, GROUP):
-                keys = keys + kin[c, d - 1, at, :]
+            keys = kp[c, 0, at, :] + kin[c, 1, at, :] + kin[c, 2, at, :]
             wide = keys * key_scale - tgt[at, c * head:(c + 1) * head].astype(jnp.float32)
             rbuf[c, :, pl.ds(pl.multiple_of(my_rows + i * 128, 128), 128)] = wide.T.astype(jnp.bfloat16)
-        own = rbuf.at[c, :, rows_of(g)]
-        for d in range(1, GROUP):
-            copy = remote(own, own, r_ss.at[c, d - 1], r_rs.at[c, d - 1], to_member(d))
-            copy.start()
-            sent.append(copy)
+        for i in range(2):
+            start(residual_copy(c, i))
+
+    def pass_residual(c):
+        residual_copy(c, 0, True).wait_recv()
+        start(residual_copy(c, 2))
 
     tile = tile_of(blk, 256)
 
+    def grad_copy(c, e):
+        return remote(gbuf.at[c, e - 1], gin.at[c, e - 1], g_ss.at[c, e - 1], g_rs.at[c, e - 1], to_quad(e))
+
     def grad_of(c):
-        for d in range(1, GROUP):
-            at = rbuf.at[c, :, rows_of(member(GROUP - d))]
-            remote(at, at, r_ss.at[c, d - 1], r_rs.at[c, d - 1], to_member(d)).wait_recv()
+        for i in (1, 2):
+            residual_copy(c, i, True).wait_recv()
         for e in list(range(1, quads)) + [0]:
             j = quad(e)
 
             def piece(i, _, j=j, e=e):
                 cols = pl.ds(pl.multiple_of(j * blk + i * tile, tile), tile)
-                gbuf[c, e, :, pl.ds(pl.multiple_of(i * tile, tile), tile)] = jnp.dot(
-                    rbuf[c], tok[:, cols], preferred_element_type=jnp.float32
-                )
+                at = pl.ds(pl.multiple_of(i * tile, tile), tile)
+                value = jnp.dot(rbuf[c], tok[:, cols], preferred_element_type=jnp.float32)
+                if e:
+                    top, low = coded(value)
+                    gbuf[c, e - 1, :head, at] = top
+                    gbuf[c, e - 1, head:, at] = low
+                else:
+                    gown[c, :, at] = value
                 return 0
 
             lax.fori_loop(0, blk // tile, piece, 0)
             if e:
-                copy = remote(gbuf.at[c, e], gin.at[c, e - 1], g_ss.at[c, e - 1], g_rs.at[c, e - 1], to_quad(e))
-                copy.start()
-                sent.append(copy)
+                start(grad_copy(c, e))
 
     def finish(c):
         if c == 0:
             more[5].wait()
             more[6].wait()
         for e in range(1, quads):
-            remote(gbuf.at[c, e], gin.at[c, e - 1], g_ss.at[c, e - 1], g_rs.at[c, e - 1], to_quad(e)).wait_recv()
+            grad_copy(c, e).wait_recv()
         cols = slice(c * head, (c + 1) * head)
 
         def piece(i, _):
             at = pl.ds(pl.multiple_of(i * 128, 128), 128)
-            total = gbuf[c, 0, :, at]
+            total = gown[c, :, at]
             for e in range(1, quads):
-                total = total + gin[c, e - 1, :, at]
+                total = total + decoded(gin[c, e - 1, :head, at], gin[c, e - 1, head:, at])
             grad = total.T * grad_scale
             stepped, mean_next, var_next = adam_update(wf[at, cols], grad, mean[at, cols], var[at, cols])
             mean[at, cols] = mean_next
@@ -290,15 +347,28 @@
         put(mean.at[:, cols], mean_o.at[:, cols])
         put(var.at[:, cols], var_o.at[:, cols])
 
-    keys_of(0)
+    key_parts(0)
+    send_keys(0)
+    if chunks > 1:
+        key_parts(1)
+    pass_keys(0)
+    if chunks > 1:
+        send_keys(1)
     for c in range(chunks):
         residual_of(c)
-        if c + 1 < chunks:
-            keys_of(c + 1)
-        grad_of(c)
-        if c >= 2:
-            finish(c - 2)
-    for c in range(max(chunks - 2, 0), chunks):
+        if 0 < c < chunks - 1:
+            pass_keys(c + 1)
+        pass_residual(c)
+        if c == 0:
+            grad_of(c)
+            if chunks > 1:
+                pass_keys(c + 1)
+        if c + 2 < chunks:
+            key_parts(c + 2)
+            send_keys(c + 2)
+        if c:
+            grad_of(c)
+    for c in range(chunks):
         finish(c)
     for copy in sent:
         copy.wait_send()
@@ -336,8 +406,9 @@
             pltpu.VMEM((chunks, GROUP, rows, head), f32),
             pltpu.VMEM((chunks, GROUP - 1, rows, head), f32),
             pltpu.VMEM((chunks, head, GROUP * rows), bf16),
-            pltpu.VMEM((chunks, quads, head, blk), f32),
-            pltpu.VMEM((chunks, quads - 1, head, blk), f32),
+            pltpu.VMEM((chunks, head, blk), f32),
+            pltpu.VMEM((chunks, quads - 1, head * 5 // 4, blk), bf16),
+            pltpu.VMEM((chunks, quads - 1, head * 5 // 4, blk), bf16),
             dma((7,)), dma((ROW_PARTS,)), dma((2 + 3 * chunks,)),
             dma((n_rep - 1,)), dma((n_rep - 1,)),
             dma((ROW_PARTS, GROUP - 1, quads)), dma((ROW_PARTS, GROUP - 1, quads)),

time: 226 us -> 207 us (0.916)
  Pallas kernels: 212 us -> 193 us
    pallas_call x1, Pallas kernels: 212 us -> 193 us  [on_device(): pl.pallas_call(functools.partial(kernel, n_rep, n_fsdp), out_shape=[state...]
where the time goes in v2:
time: 207 us; the launch traced here: 206 us
  Pallas kernels  193 us (93%)
  local copies, waits for them, and re-layouts  11.6 us (6%)
    pallas_call x1, Pallas kernels, on_device(): pl.pallas_call(functools.partial(kernel, n_rep, n_fsdp), out_shape=[state...  193 us
    unnamed x13, local copies, waits for them, and re-layouts  11.6 us

profile of v2, /device:TPU:0, one launch (start us, length us, event | category | flops | bytes accessed | tf_op | source)
XLA Modules:
  0.0 206.4 jit_solution(6165061866298337449)
XLA Ops:
  1.9 192.9 %shard_map.137 = (f32[1024,512]{1,0:T(8,128)}, f32[1024,512]{1,0:T(8,128)}, f32[1024,512]{1,0:T(8,128)}, f32[1024,512]{1,0:T(8,128)}, f32[1024,512]{1,0:T(8,128)}) custom-call(s32[1]{0:T(128)} %bitcast.10.frag_ref, s32[1]{0:T(128)S(6)} %copy.21.delay_ref, bf16[384,8192]{1,0:T(8,128)(2,1)} %bitcast.14, bf16[384,512]{1,0:T(8,128)(2,1)} %bitcast.19, ...), custom_call_target="tpu_custom_call" | custom-call | flops 6442450944 | bytes 27262976 | tf_op jit(solution)/shard_map/pallas_call | solution.py:390
  194.8 0.0 copy-start.3
  194.8 3.2 %copy.22 = f32[1,1024,512]{2,1,0:T(8,128)} copy(f32[1,1024,512]{2,1,0:T(8,128)} %bitcast.13) | data formatting | bytes 4194304
  198.0 0.0 copy-done.3
  198.1 0.0 copy-start.2
  198.1 1.3 copy.23
  199.4 1.0 copy-done.2
  200.4 0.0 copy-start.1
  200.4 1.3 copy.24
  201.7 1.0 copy-done.1
  202.7 0.0 copy-start
  202.8 1.3 copy.25
  204.1 1.0 copy-done
  205.1 1.3 copy.26
Async XLA Ops:
  194.8 3.2 %copy-start.3 = (f32[1024,512]{1,0:T(8,128)S(1)}, f32[1024,512]{1,0:T(8,128)}, u32[]{:S(2)}) copy-start(f32[1024,512]{1,0:T(8,128)} %get-tuple-element.11) | copy-start | bytes 6291460
  198.1 2.3 %copy-start.2 = (f32[1024,512]{1,0:T(8,128)S(1)}, f32[1024,512]{1,0:T(8,128)}, u32[]{:S(2)}) copy-start(f32[1024,512]{1,0:T(8,128)} %get-tuple-element.12) | copy-start | bytes 6291460
  200.4 2.3 %copy-start.1 = (f32[1024,512]{1,0:T(8,128)S(1)}, f32[1024,512]{1,0:T(8,128)}, u32[]{:S(2)}) copy-start(f32[1024,512]{1,0:T(8,128)} %get-tuple-element.23) | copy-start | bytes 6291460
  202.7 2.3 %copy-start = (f32[1024,512]{1,0:T(8,128)S(1)}, f32[1024,512]{1,0:T(8,128)}, u32[]{:S(2)}) copy-start(f32[1024,512]{1,0:T(8,128)} %get-tuple-element.24) | copy-start | bytes 6291460
